TPU v7x, 32 devices: a whole 2x2x4 slice. The times are simulated.
32 devices in a mesh: row: 4 (over z), col: 8 (over y, x, core).
Axes of the slice: x: 2, y: 2, z: 4, core: 2. Of those that a mesh axis runs over, the one named last changes fastest.
Arguments:
- embeddings: bfloat16 [4096, 768], P(('row', 'col')), may hold values from -4 to 4
- neg_ids: int32 [4, 2048], P('row', 'col'), may hold values from 0 to 16383, as said below
- neg_counts: int32 [4], P('row'), may hold values from 256 to 2048, as said below
- index_rows: bfloat16 [16384, 768], P('row'), may hold values from -4 to 4
Outputs:
- row_loss: float32 [4096], P(('row', 'col'))
- grad: float32 [4096, 768], P(('row', 'col'))
Inputs may be any that keep to these rules, and one draw needn't show every extreme that they name: `neg_counts`: every entry lies within the range; some lists are full (2048) and some hold exactly 256 entries. Index shard of an id is id // 4096. Among the 256 slots of one device (neg_ids[b, c * 256 : (c + 1) * 256]) at most 128 ids belong to any one index shard, and in every such run exactly 128 belong to one of them.
All inputs are finite; a program needn't handle non-finite values.
Results may differ from a plain program's by a relative error of at most 0.00059.
Values may be sent and summed in bfloat16 or wider, within the bound.
A program may use at most 128 MiB of HBM per device.

v0:
```python
import jax
import jax.numpy as jnp
from jax import lax
from jax.sharding import PartitionSpec as P

D = 768


def per_device(embeddings, neg_ids, neg_counts, index_rows):
    scale = D ** (-0.5)
    n_col = lax.axis_size("col")
    shard_rows = embeddings.shape[0]
    width = embeddings.shape[1]
    row_id = lax.axis_index("row")
    col_id = lax.axis_index("col")
    queries = lax.all_gather(embeddings, "col", axis=0, tiled=True)
    keys = lax.all_gather(embeddings, "row", axis=0, tiled=True)
    query_count = queries.shape[0]
    key_count = keys.shape[0]
    requests = lax.all_gather(neg_ids, "row", axis=0, tiled=True)
    owned_count = index_rows.shape[0]
    slot_count = neg_ids.shape[1]
    local_ids = requests - row_id * owned_count
    owned = (local_ids >= 0) & (local_ids < owned_count)
    picked = jnp.take(index_rows, jnp.clip(local_ids, 0, owned_count - 1), axis=0)
    picked = jnp.where(owned[..., None], picked, jnp.zeros_like(picked))
    fetched = lax.psum_scatter(
        picked.astype(jnp.float32).astype(jnp.bfloat16), "row", scatter_dimension=0, tiled=True
    ).astype(jnp.float32)
    negatives = fetched[0].astype(jnp.bfloat16)
    row_glob = row_id * query_count + jnp.arange(query_count, dtype=jnp.int32)
    key_local = jnp.arange(key_count, dtype=jnp.int32)
    col_glob = (key_local // shard_rows * n_col + col_id) * shard_rows + key_local % shard_rows
    scores = jnp.dot(queries, keys.T, preferred_element_type=jnp.float32) * scale
    scores = jnp.where(row_glob[:, None] == col_glob[None, :], -jnp.inf, scores)
    slot_glob = col_id * slot_count + jnp.arange(slot_count, dtype=jnp.int32)
    hard = jnp.dot(queries, negatives.T, preferred_element_type=jnp.float32) * scale
    hard = jnp.where((slot_glob < neg_counts[0])[None, :], hard, -jnp.inf)
    local_top = jnp.maximum(jnp.max(scores, axis=1), jnp.max(hard, axis=1))
    top = lax.pmax(local_top, "col")
    partial_value = jnp.sum(jnp.exp(scores - top[:, None]), axis=1) + jnp.sum(
        jnp.exp(hard - top[:, None]), axis=1
    )
    total = lax.psum(partial_value, "col")
    lse = top + jnp.log(total)
    own_f = embeddings.astype(jnp.float32)
    partner = own_f.reshape(shard_rows // 2, 2, width)[:, ::-1].reshape(shard_rows, width)
    positive = jnp.sum(own_f * partner, axis=1) * scale
    own_lse = lax.dynamic_slice_in_dim(lse, col_id * shard_rows, shard_rows, 0)
    row_loss = own_lse - positive
    target = (jnp.bitwise_xor(row_glob, 1)[:, None] == col_glob[None, :]).astype(jnp.float32)
    probs_grad = (jnp.exp(scores - lse[:, None]) - target).astype(jnp.bfloat16)
    hard_probs = jnp.exp(hard - lse[:, None]).astype(jnp.bfloat16)
    term = jnp.dot(probs_grad, keys, preferred_element_type=jnp.float32)
    query_part = lax.psum_scatter(
        term + jnp.dot(hard_probs, negatives, preferred_element_type=jnp.float32),
        "col",
        scatter_dimension=0,
        tiled=True,
    )
    key_part = lax.psum_scatter(
        lax.dot_general(
            probs_grad, queries, (((0,), (0,)), ((), ())), preferred_element_type=jnp.float32
        ),
        "row",
        scatter_dimension=0,
        tiled=True,
    )
    grad = query_part + key_part
    return (row_loss, grad)


def solution(mesh):
    return jax.shard_map(
        per_device,
        mesh=mesh,
        in_specs=(P(("row", "col"), None), P("row", "col"), P("row"), P("row", None)),
        out_specs=(P(("row", "col")), P(("row", "col"), None)),
        check_vma=False,
    )
```

profile of v0, /device:TPU:0, one launch (start us, length us, event | category | flops | bytes accessed | tf_op | source)
XLA Modules:
  0.0 196.2 jit_solution(175145558935563326)
XLA Ops:
  8.0 0.7 all-gather.3.cloned.1.call-update
  8.8 12.8 %all-gather = s32[4,1,256]{2,1,0:T(1,128)S(1)} all-gather(s32[1,1,256]{2,1,0:T(1,128)} %bitcast.31), channel_id=1, replica_groups=mesh['row'=4,'col'=8] {'row'}, dimensions={0}, use_global_device_ids=true | all-gather | bytes 5120 | tf_op jit(solution)/shard_map/all_gather | solution.py:20
  21.7 8.1 %gather_fusion = bf16[1024,768]{1,0:T(8,128)(2,1)S(1)} fusion(bf16[4096,768]{1,0:T(8,128)(2,1)} %param.7, s32[1024]{0:T(1024)S(1)} %broadcast_clamp_fusion), kind=kCustom, calls=%fused_computation | custom fusion | bytes 3149824 | tf_op jit(solution)/shard_map/jit(_take)/gather | solution.py:25
  29.8 1.4 select_select_fusion
  32.0 26.3 %all_gather.10 = bf16[512,768]{1,0:T(8,128)(2,1)S(1)} all-gather(bf16[128,768]{1,0:T(8,128)(2,1)S(1)} %copy-done), channel_id=1, replica_groups=mesh['row'=4,'col'=8] {'row'}, dimensions={0}, use_global_device_ids=true | all-gather | bytes 983040 | tf_op jit(solution)/shard_map/all_gather | solution.py:17
  58.3 2.7 %fusion.18 = (f32[1024]{0:T(1024)S(1)}, f32[1024,512]{0,1:T(8,128)S(1)}) fusion(bf16[1024,768]{1,0:T(8,128)(2,1)} %all-gather.3.cloned.1.call-done, bf16[512,768]{1,0:T(8,128)(2,1)S(1)} %all_gather.10, s32[512]{0:T(512)S(1)} %fusion.12, s32[1024]{0:T(1024)S(1)} %iota_add_fusion), kind=kOutput, calls=%fused_computation.43 | convolution fusion | flops 807402496 | bytes 4466688 | tf_op jit(solution)/shard_map/dot_general | solution.py:34
  61.0 12.1 %reduce-scatter.4.cloned.1.call-done = bf16[1,256,768]{2,1,0:T(8,128)(2,1)} async-done(((bf16[4,256,768]{2,1,0:T(8,128)(2,1)}), bf16[1,256,768]{2,1,0:T(8,128)(2,1)}) %reduce-scatter.4.cloned.1.call-update) | async-done | bytes 393232 | tf_op jit(solution)/shard_map/reduce_scatter | solution.py:27
  73.1 2.2 %fusion.19 = (f32[1024]{0:T(1024)S(1)}, f32[256,1024]{1,0:T(8,128)S(1)}) fusion(bf16[1024,768]{1,0:T(8,128)(2,1)} %all-gather.3.cloned.1.call-done, bf16[1,256,768]{2,1,0:T(8,128)(2,1)} %reduce-scatter.4.cloned.1.call-done, pred[256]{0:T(512)(128)(4,1)S(1)} %add_compare_fusion), kind=kOutput, calls=%fused_computation.44 | convolution fusion | flops 403438592 | bytes 3019008 | tf_op jit(solution)/shard_map/dot_general | solution.py:37
  75.3 14.0 %pmax.7 = f32[1024]{0:T(1024)S(1)} all-reduce(f32[1024]{0:T(1024)S(1)} %max.9), channel_id=1, replica_groups=mesh['row'=4,'col'=8] {'col'}, use_global_device_ids=true, to_apply=%region_3.4 | all-reduce | flops 1024 | bytes 8192 | tf_op jit(solution)/shard_map/pmax | solution.py:40
  89.2 0.2 exponential_reduce_fusion.1
  89.4 0.3 exponential_reduce_fusion
  89.7 11.8 %psum.7 = f32[1024]{0:T(1024)S(1)} all-reduce(f32[1024]{0:T(1024)S(1)} %add.93), channel_id=1, replica_groups=mesh['row'=4,'col'=8] {'col'}, use_global_device_ids=true, to_apply=%region_6.7 | all-reduce | flops 1024 | bytes 8192 | tf_op jit(solution)/shard_map/psum | solution.py:44
  101.5 3.8 %fusion.16 = f32[512,768]{1,0:T(8,128)} fusion(bf16[1024,768]{1,0:T(8,128)(2,1)} %all-gather.3.cloned.1.call-done, f32[1024,512]{0,1:T(8,128)S(1)} %get-tuple-element.3, s32[1024]{0:T(1024)S(1)} %broadcast_xor_fusion, f32[1024]{0:T(1024)S(1)} %log_add_fusion, s32[512]{0:T(512)S(1)} %fusion.12), kind=kOutput, calls=%fused_computation.41 | convolution fusion | flops 807927808 | bytes 5253120 | tf_op jit(solution)/shard_map/dot_general | solution.py:62
  105.3 0.0 reduce-scatter.6.cloned.1.call-start
  105.4 2.3 %fusion.17 = f32[1024,768]{1,0:T(8,128)S(1)} fusion(bf16[512,768]{1,0:T(8,128)(2,1)} %copy-done.1, f32[1024,512]{0,1:T(8,128)S(1)} %get-tuple-element.3, s32[1024]{0:T(1024)S(1)} %broadcast_xor_fusion, f32[1024]{0:T(1024)S(1)} %log_add_fusion, s32[512]{0:T(512)S(1)} %fusion.12), kind=kOutput, calls=%fused_computation.42 | convolution fusion | flops 807927808 | bytes 6039552 | tf_op jit(solution)/shard_map/dot_general | solution.py:54
  107.7 2.3 %convolution_add_fusion = f32[1024,768]{1,0:T(8,128)} fusion(f32[1024,768]{1,0:T(8,128)S(1)} %fusion.17, f32[256,1024]{1,0:T(8,128)S(1)} %get-tuple-element.5, f32[1024]{0:T(1024)S(1)} %log_add_fusion, bf16[1,256,768]{2,1,0:T(8,128)(2,1)S(1)} %copy-done.2), kind=kOutput, calls=%fused_computation.4 | convolution fusion | flops 403963904 | bytes 7737344 | tf_op jit(solution)/shard_map/dot_general | solution.py:56
  110.0 0.2 reshape.55
  110.2 1.1 rev.3
  111.4 0.3 reshape.56
  111.6 0.1 multiply_reduce_fusion
  111.8 0.6 multiply_subtract_fusion
  112.3 26.1 %reduce-scatter.8.cloned.1.call-done = f32[128,768]{1,0:T(8,128)} async-done(((f32[512,768]{1,0:T(8,128)}), f32[128,768]{1,0:T(8,128)}) %reduce-scatter.8.cloned.1.call-update) | async-done | bytes 393232 | tf_op jit(solution)/shard_map/reduce_scatter | solution.py:61
  138.4 48.2 %reduce-scatter.6.cloned.1.call-done = f32[128,768]{1,0:T(8,128)} async-done(((f32[1024,768]{1,0:T(8,128)}), f32[128,768]{1,0:T(8,128)}) %reduce-scatter.6.cloned.1.call-update) | async-done | bytes 393232 | tf_op jit(solution)/shard_map/reduce_scatter | solution.py:55
  186.7 1.9 add.97
  (27 shorter events, 0.3 us)
Async XLA Ops:
  8.0 50.3 %all-gather.3.cloned.1.call-start = ((), (), s32[]{:S(2)}) async-start(), calls=%async_computation.3 | async-start | bytes 1769472 | tf_op jit(solution)/shard_map/all_gather | solution.py:16
  8.7 64.4 %reduce-scatter.4.cloned.1.call-start = ((), (), s32[]{:S(2)}) async-start(), calls=%async_computation.4 | async-start | bytes 1966080 | tf_op jit(solution)/shard_map/reduce_scatter | solution.py:27
  29.8 2.2 %copy-start = (bf16[128,768]{1,0:T(8,128)(2,1)S(1)}, bf16[128,768]{1,0:T(8,128)(2,1)}, u32[]{:S(2)}) copy-start(bf16[128,768]{1,0:T(8,128)(2,1)} %param.4) | copy-start | bytes 589828
  31.2 107.2 %reduce-scatter.8.cloned.1.call-start = ((), (), s32[]{:S(2)}) async-start(), calls=%async_computation.6 | async-start | bytes 1966080 | tf_op jit(solution)/shard_map/reduce_scatter | solution.py:61
  58.3 2.7 %copy-start.1 = (bf16[512,768]{1,0:T(8,128)(2,1)}, bf16[512,768]{1,0:T(8,128)(2,1)S(1)}, u32[]{:S(2)}) copy-start(bf16[512,768]{1,0:T(8,128)(2,1)S(1)} %all_gather.10) | copy-start | bytes 2359300
  105.3 81.4 %reduce-scatter.6.cloned.1.call-start = ((), (), s32[]{:S(2)}) async-start(), calls=%async_computation.5 | async-start | bytes 3538944 | tf_op jit(solution)/shard_map/reduce_scatter | solution.py:55
  105.4 2.3 %copy-start.2 = (bf16[1,256,768]{2,1,0:T(8,128)(2,1)S(1)}, bf16[1,256,768]{2,1,0:T(8,128)(2,1)}, u32[]{:S(2)}) copy-start(bf16[1,256,768]{2,1,0:T(8,128)(2,1)} %reduce-scatter.4.cloned.1.call-done) | copy-start | bytes 1179652
Sparse Core Ops, SparseCore 0:
  10.7 28.4 all-gather.2
Sparse Core Ops, SparseCore 1:
  31.3 41.7 reduce-scatter.3
  105.4 33.0 reduce-scatter.7
  141.7 44.9 reduce-scatter.5
where the time goes:
time: 197 us; the launch traced here: 196 us
  waiting for transfers between devices  87.1 us (44%)
  blocking collectives  64.9 us (33%)
  between operations  16.5 us (8%)
  matrix products  13.3 us (7%)
  local copies, waits for them, and re-layouts  9.65 us (5%)
  other arithmetic  4.59 us (2%)
    reduce_scatter x1, waiting for transfers between devices, per_device(): lax.psum_scatter(term + jnp.dot(hard_probs, negatives, preferred_element_...  48.2 us
    all_gather x1, blocking collectives, per_device(): keys = lax.all_gather(embeddings, 'row', axis=0, tiled=True)  26.3 us
    reduce_scatter x1, waiting for transfers between devices, per_device(): lax.psum_scatter(lax.dot_general(probs_grad, queries, (((0,), (0,)), ((),...  26.1 us
    pmax x1, blocking collectives, per_device(): top = lax.pmax(local_top, 'col')  14 us
    all_gather x1, blocking collectives, per_device(): requests = lax.all_gather(neg_ids, 'row', axis=0, tiled=True)  12.8 us
    reduce_scatter x1, waiting for transfers between devices, per_device(): lax.psum_scatter(picked.astype(jnp.float32).astype(jnp.bfloat16), 'row',...  12.1 us
    psum x1, blocking collectives, per_device(): total = lax.psum(partial_value, 'col')  11.8 us
    gather x1, local copies, waits for them, and re-layouts, per_device(): jnp.take(index_rows, jnp.clip(local_ids, 0, owned_count - 1), axis=0)  8.07 us
  transfers between devices with their start and end apart: 4, of which 3 were waited for; matrix products, arithmetic and copies ran while one was open for 10% of the time, Pallas kernels for 0%

commit v1 on v0

--- a/solution.py
+++ b/solution.py
@@ -41,7 +41,9 @@
     partial_value = jnp.sum(jnp.exp(scores - top[:, None]), axis=1) + jnp.sum(
         jnp.exp(hard - top[:, None]), axis=1
     )
-    total = lax.psum(partial_value, "col")
+    total = partial_value
+    for hop in (1, 2, 4):
+        total = total + lax.ppermute(total, "col", [(dev, dev ^ hop) for dev in range(8)])
     lse = top + jnp.log(total)
     own_f = embeddings.astype(jnp.float32)
     partner = own_f.reshape(shard_rows // 2, 2, width)[:, ::-1].reshape(shard_rows, width)

time: 197 us -> 192 us (0.975)
  blocking collectives: 64.9 us -> 53.1 us
  waiting for transfers between devices: 87.1 us -> 95 us
    psum x1 -> x0, blocking collectives: 11.8 us -> none  [per_device(): total = lax.psum(partial_value, 'col')]
    ppermute x0 -> x3, waiting for transfers between devices: none -> 7.88 us  [per_device(): lax.ppermute(total, 'col', [(dev, dev ^ hop) for dev in range(8)])]
  transfers between devices with their start and end apart: 4 -> 7, of which waited for: 3 -> 6; matrix products, arithmetic and copies ran while one was open for 10% -> 10% of each run, Pallas kernels for 0% -> 0%
where the time goes in v1:
time: 192 us; the launch traced here: 191 us
  waiting for transfers between devices  95 us (49%)
  blocking collectives  53.1 us (28%)
  between operations  16.5 us (9%)
  matrix products  11.9 us (6%)
  local copies, waits for them, and re-layouts  9.66 us (5%)
  other arithmetic  4.57 us (2%)
    reduce_scatter x1, waiting for transfers between devices, per_device(): lax.psum_scatter(term + jnp.dot(hard_probs, negatives, preferred_element_...  48.2 us
    all_gather x1, blocking collectives, per_device(): keys = lax.all_gather(embeddings, 'row', axis=0, tiled=True)  26.3 us
    reduce_scatter x1, waiting for transfers between devices, per_device(): lax.psum_scatter(lax.dot_general(probs_grad, queries, (((0,), (0,)), ((),...  26.1 us
    pmax x1, blocking collectives, per_device(): top = lax.pmax(local_top, 'col')  14 us
    all_gather x1, blocking collectives, per_device(): requests = lax.all_gather(neg_ids, 'row', axis=0, tiled=True)  12.8 us
    reduce_scatter x1, waiting for transfers between devices, per_device(): lax.psum_scatter(picked.astype(jnp.float32).astype(jnp.bfloat16), 'row',...  12.1 us
    gather x1, local copies, waits for them, and re-layouts, per_device(): jnp.take(index_rows, jnp.clip(local_ids, 0, owned_count - 1), axis=0)  8.07 us
    ppermute x3, waiting for transfers between devices, per_device(): lax.ppermute(total, 'col', [(dev, dev ^ hop) for dev in range(8)])  7.88 us
  transfers between devices with their start and end apart: 7, of which 6 were waited for; matrix products, arithmetic and copies ran while one was open for 10% of the time, Pallas kernels for 0%

profile of v1, /device:TPU:0, one launch (start us, length us, event | category | flops | bytes accessed | tf_op | source)
XLA Modules:
  0.0 191.4 jit_solution(9554369878068623590)
XLA Ops:
  8.0 0.7 all-gather.3.cloned.1.call-update
  8.8 12.8 %all-gather = s32[4,1,256]{2,1,0:T(1,128)S(1)} all-gather(s32[1,1,256]{2,1,0:T(1,128)} %bitcast.31), channel_id=1, replica_groups=mesh['row'=4,'col'=8] {'row'}, dimensions={0}, use_global_device_ids=true | all-gather | bytes 5120 | tf_op jit(solution)/shard_map/all_gather | solution.py:20
  21.7 8.1 %gather_fusion = bf16[1024,768]{1,0:T(8,128)(2,1)S(1)} fusion(bf16[4096,768]{1,0:T(8,128)(2,1)} %param.7, s32[1024]{0:T(1024)S(1)} %broadcast_clamp_fusion), kind=kCustom, calls=%fused_computation | custom fusion | bytes 3149824 | tf_op jit(solution)/shard_map/jit(_take)/gather | solution.py:25
  29.8 1.4 select_select_fusion
  32.0 26.3 %all_gather.10 = bf16[512,768]{1,0:T(8,128)(2,1)S(1)} all-gather(bf16[128,768]{1,0:T(8,128)(2,1)S(1)} %copy-done), channel_id=1, replica_groups=mesh['row'=4,'col'=8] {'row'}, dimensions={0}, use_global_device_ids=true | all-gather | bytes 983040 | tf_op jit(solution)/shard_map/all_gather | solution.py:17
  58.2 2.7 %fusion.18 = (f32[1024]{0:T(1024)S(1)}, f32[1024,512]{0,1:T(8,128)S(1)}) fusion(bf16[1024,768]{1,0:T(8,128)(2,1)} %all-gather.3.cloned.1.call-done, bf16[512,768]{1,0:T(8,128)(2,1)S(1)} %all_gather.10, s32[512]{0:T(512)S(1)} %fusion.12, s32[1024]{0:T(1024)S(1)} %iota_add_fusion), kind=kOutput, calls=%fused_computation.43 | convolution fusion | flops 807402496 | bytes 4466688 | tf_op jit(solution)/shard_map/dot_general | solution.py:34
  61.0 12.1 %reduce-scatter.4.cloned.1.call-done = bf16[1,256,768]{2,1,0:T(8,128)(2,1)} async-done(((bf16[4,256,768]{2,1,0:T(8,128)(2,1)}), bf16[1,256,768]{2,1,0:T(8,128)(2,1)}) %reduce-scatter.4.cloned.1.call-update) | async-done | bytes 393232 | tf_op jit(solution)/shard_map/reduce_scatter | solution.py:27
  73.0 2.2 %fusion.19 = (f32[1024]{0:T(1024)S(1)}, f32[256,1024]{1,0:T(8,128)S(1)}) fusion(bf16[1024,768]{1,0:T(8,128)(2,1)} %all-gather.3.cloned.1.call-done, bf16[1,256,768]{2,1,0:T(8,128)(2,1)} %reduce-scatter.4.cloned.1.call-done, pred[256]{0:T(512)(128)(4,1)S(1)} %add_compare_fusion), kind=kOutput, calls=%fused_computation.44 | convolution fusion | flops 403438592 | bytes 3019008 | tf_op jit(solution)/shard_map/dot_general | solution.py:37
  75.2 14.0 %pmax.7 = f32[1024]{0:T(1024)S(1)} all-reduce(f32[1024]{0:T(1024)S(1)} %max.9), channel_id=1, replica_groups=mesh['row'=4,'col'=8] {'col'}, use_global_device_ids=true, to_apply=%region_3.4 | all-reduce | flops 1024 | bytes 8192 | tf_op jit(solution)/shard_map/pmax | solution.py:40
  89.4 0.3 exponential_reduce_fusion
  89.8 1.2 collective-permute-done
  90.9 3.6 %collective-permute-done.1 = f32[1024]{0:T(1024)S(1)} collective-permute-done((f32[1024]{0:T(1024)S(1)}, f32[1024]{0:T(1024)S(1)}, u32[]{:S(2)}, u32[]{:S(2)}) %collective-permute-start.1) | collective-permute-done | bytes 4128 | tf_op jit(solution)/shard_map/ppermute | solution.py:46
  94.5 0.5 collective-permute-start.2
  95.0 3.1 %collective-permute-done.2 = f32[1024]{0:T(1024)S(1)} collective-permute-done((f32[1024]{0:T(1024)S(1)}, f32[1024]{0:T(1024)S(1)}, u32[]{:S(2)}, u32[]{:S(2)}) %collective-permute-start.2) | collective-permute-done | bytes 4128 | tf_op jit(solution)/shard_map/ppermute | solution.py:46
  98.2 2.4 %fusion.16 = f32[512,768]{1,0:T(8,128)} fusion(bf16[1024,768]{1,0:T(8,128)(2,1)S(1)} %copy-done.3, f32[1024,512]{0,1:T(8,128)S(1)} %get-tuple-element.3, s32[1024]{0:T(1024)S(1)} %broadcast_xor_fusion, f32[1024]{0:T(1024)S(1)} %log_add_fusion, s32[512]{0:T(512)S(1)} %fusion.12), kind=kOutput, calls=%fused_computation.41 | convolution fusion | flops 807927808 | bytes 5253120 | tf_op jit(solution)/shard_map/dot_general | solution.py:64
  100.6 2.3 %fusion.17 = f32[1024,768]{1,0:T(8,128)S(1)} fusion(bf16[512,768]{1,0:T(8,128)(2,1)} %copy-done.1, f32[1024,512]{0,1:T(8,128)S(1)} %get-tuple-element.3, s32[1024]{0:T(1024)S(1)} %broadcast_xor_fusion, f32[1024]{0:T(1024)S(1)} %log_add_fusion, s32[512]{0:T(512)S(1)} %fusion.12), kind=kOutput, calls=%fused_computation.42 | convolution fusion | flops 807927808 | bytes 6039552 | tf_op jit(solution)/shard_map/dot_general | solution.py:56
  103.0 2.3 %convolution_add_fusion = f32[1024,768]{1,0:T(8,128)} fusion(f32[1024,768]{1,0:T(8,128)S(1)} %fusion.17, f32[256,1024]{1,0:T(8,128)S(1)} %get-tuple-element.5, f32[1024]{0:T(1024)S(1)} %log_add_fusion, bf16[1,256,768]{2,1,0:T(8,128)(2,1)S(1)} %copy-done.2), kind=kOutput, calls=%fused_computation.4 | convolution fusion | flops 403963904 | bytes 7737344 | tf_op jit(solution)/shard_map/dot_general | solution.py:58
  105.3 0.2 reshape.55
  105.5 1.1 rev.3
  106.6 0.3 reshape.56
  107.0 0.6 multiply_subtract_fusion
  107.6 26.1 %reduce-scatter.8.cloned.1.call-done = f32[128,768]{1,0:T(8,128)} async-done(((f32[512,768]{1,0:T(8,128)}), f32[128,768]{1,0:T(8,128)}) %reduce-scatter.8.cloned.1.call-update) | async-done | bytes 393232 | tf_op jit(solution)/shard_map/reduce_scatter | solution.py:63
  133.7 48.2 %reduce-scatter.6.cloned.1.call-done = f32[128,768]{1,0:T(8,128)} async-done(((f32[1024,768]{1,0:T(8,128)}), f32[128,768]{1,0:T(8,128)}) %reduce-scatter.6.cloned.1.call-update) | async-done | bytes 393232 | tf_op jit(solution)/shard_map/reduce_scatter | solution.py:57
  181.9 1.9 add.107
  (36 shorter events, 0.7 us)
Async XLA Ops:
  8.0 50.2 %all-gather.3.cloned.1.call-start = ((), (), s32[]{:S(2)}) async-start(), calls=%async_computation.3 | async-start | bytes 1769472 | tf_op jit(solution)/shard_map/all_gather | solution.py:16
  8.7 64.3 %reduce-scatter.4.cloned.1.call-start = ((), (), s32[]{:S(2)}) async-start(), calls=%async_computation.4 | async-start | bytes 1966080 | tf_op jit(solution)/shard_map/reduce_scatter | solution.py:27
  29.8 2.1 %copy-start = (bf16[128,768]{1,0:T(8,128)(2,1)S(1)}, bf16[128,768]{1,0:T(8,128)(2,1)}, u32[]{:S(2)}) copy-start(bf16[128,768]{1,0:T(8,128)(2,1)} %param.4) | copy-start | bytes 589828
  31.2 102.5 %reduce-scatter.8.cloned.1.call-start = ((), (), s32[]{:S(2)}) async-start(), calls=%async_computation.6 | async-start | bytes 1966080 | tf_op jit(solution)/shard_map/reduce_scatter | solution.py:63
  58.2 2.7 %copy-start.1 = (bf16[512,768]{1,0:T(8,128)(2,1)}, bf16[512,768]{1,0:T(8,128)(2,1)S(1)}, u32[]{:S(2)}) copy-start(bf16[512,768]{1,0:T(8,128)(2,1)S(1)} %all_gather.10) | copy-start | bytes 2359300
  89.2 9.0 %copy-start.3 = (bf16[1024,768]{1,0:T(8,128)(2,1)S(1)}, bf16[1024,768]{1,0:T(8,128)(2,1)}, u32[]{:S(2)}) copy-start(bf16[1024,768]{1,0:T(8,128)(2,1)} %all-gather.3.cloned.1.call-done) | copy-start | bytes 4718596
  89.7 1.2 collective-permute-start
  90.9 3.6 %collective-permute-start.1 = (f32[1024]{0:T(1024)S(1)}, f32[1024]{0:T(1024)S(1)}, u32[]{:S(2)}, u32[]{:S(2)}) collective-permute-start(f32[1024]{0:T(1024)S(1)} %add.101), channel_id=1, source_target_pairs={{0,2},{1,3},{2,0},{3,1},{4,6},{5,7},{6,4},{7,5},{8,10},{9,11},{10,... | collective-permute-start | bytes 12296 | tf_op jit(solution)/shard_map/ppermute | solution.py:46
  94.5 3.6 %collective-permute-start.2 = (f32[1024]{0:T(1024)S(1)}, f32[1024]{0:T(1024)S(1)}, u32[]{:S(2)}, u32[]{:S(2)}) collective-permute-start(f32[1024]{0:T(1024)S(1)} %add.102), channel_id=1, source_target_pairs={{0,4},{1,5},{2,6},{3,7},{4,0},{5,1},{6,2},{7,3},{8,12},{9,13},{10,... | collective-permute-start | bytes 12296 | tf_op jit(solution)/shard_map/ppermute | solution.py:46
  100.6 81.4 %reduce-scatter.6.cloned.1.call-start = ((), (), s32[]{:S(2)}) async-start(), calls=%async_computation.5 | async-start | bytes 3538944 | tf_op jit(solution)/shard_map/reduce_scatter | solution.py:57
  100.6 2.3 %copy-start.2 = (bf16[1,256,768]{2,1,0:T(8,128)(2,1)S(1)}, bf16[1,256,768]{2,1,0:T(8,128)(2,1)}, u32[]{:S(2)}) copy-start(bf16[1,256,768]{2,1,0:T(8,128)(2,1)} %reduce-scatter.4.cloned.1.call-done) | copy-start | bytes 1179652
Sparse Core Ops, SparseCore 0:
  10.7 28.4 all-gather.2
Sparse Core Ops, SparseCore 1:
  31.3 41.7 reduce-scatter.3
  100.7 33.0 reduce-scatter.7
  137.0 44.9 reduce-scatter.5
